TPU v7x, 512 devices: a whole 4x8x8 slice. The times are simulated.
512 devices in a mesh: gx: 32 (over x_hi, y, core), gy: 16 (over x_lo, z).
Axes of the slice: x: 4 (x_hi: 2, x_lo: 2; x = x_hi * 2 + x_lo), y: 8, z: 8, core: 2. Of those that a mesh axis runs over, the one named last changes fastest.
Arguments:
- tokens: bfloat16 [256, 18432], P('gy', 'gx'), may hold values from -6 to 6
- gate_weight: bfloat16 [18432, 9216], P('gx', 'gy'), may hold values from -0.046875 to 0.046875
- up_weight: bfloat16 [18432, 9216], P('gx', 'gy'), may hold values from -0.046875 to 0.046875
- down_weight: bfloat16 [9216, 18432], P('gy', 'gx'), may hold values from -0.0625 to 0.0625
- cotangent: bfloat16 [256, 18432], P('gy', 'gx'), may hold values from -2.796875 to 2.796875
Outputs:
- output: bfloat16 [256, 18432], P('gy', 'gx')
- input_grad: bfloat16 [256, 18432], P('gy', 'gx')
- gate_grad: bfloat16 [18432, 9216], P('gx', 'gy')
- up_grad: bfloat16 [18432, 9216], P('gx', 'gy')
- down_grad: bfloat16 [9216, 18432], P('gy', 'gx')
All inputs are finite; a program needn't handle non-finite values.
Results may differ from a plain program's by a relative error of at most 0.0049.
Values may be sent and summed in bfloat16 or wider, within the bound.
A program may use at most 64 MiB of HBM per device.

v0:
```python
import jax
import jax.numpy as jnp
from jax import lax
from jax.sharding import PartitionSpec as P


def contract_last(left, right):
    return lax.dot_general(
        left, right, (((1,), (1,)), ((), ())), preferred_element_type=jnp.float32
    )


def contract_first(left, right):
    return lax.dot_general(
        left, right, (((0,), (0,)), ((), ())), preferred_element_type=jnp.float32
    )


def gating(gate, up):
    sigmoid_gate = jax.nn.sigmoid(gate)
    activated = gate * sigmoid_gate
    return (sigmoid_gate, activated, (activated * up).astype(jnp.bfloat16))


def deltas(hidden_grad, gate, up):
    sigmoid_gate = jax.nn.sigmoid(gate)
    activated = gate * sigmoid_gate
    gate_delta = (hidden_grad * up * sigmoid_gate * (1.0 + gate * (1.0 - sigmoid_gate))).astype(
        jnp.bfloat16
    )
    up_delta = (hidden_grad * activated).astype(jnp.bfloat16)
    return (gate_delta, up_delta)


def shards(tokens, gate_weight, up_weight, down_weight, cotangent):
    features, grad_rows = (
        lax.all_gather(tokens, "gy", axis=0, tiled=True),
        lax.all_gather(cotangent, "gy", axis=0, tiled=True),
    )
    hidden_width = gate_weight.shape[1]
    block = features
    first = jnp.dot(block, gate_weight, preferred_element_type=jnp.float32)
    second = jnp.dot(block, up_weight, preferred_element_type=jnp.float32)
    joined = lax.psum_scatter(
        jnp.concatenate([first, second], axis=1), "gx", scatter_dimension=0, tiled=True
    )
    gate = joined[:, :hidden_width]
    up = joined[:, hidden_width:]
    sigmoid_gate, activated, hidden_share = gating(gate, up)
    hidden = lax.all_gather(hidden_share, "gx", axis=0, tiled=True)
    block = hidden
    output = lax.psum_scatter(
        jnp.dot(block, down_weight, preferred_element_type=jnp.float32),
        "gy",
        scatter_dimension=0,
        tiled=True,
    ).astype(jnp.bfloat16)
    block = grad_rows
    hidden_grad = lax.psum_scatter(
        contract_last(block, down_weight), "gx", scatter_dimension=0, tiled=True
    )
    gate_share, up_share = deltas(hidden_grad, gate, up)
    gate_delta, up_delta = (
        lax.all_gather(gate_share, "gx", axis=0, tiled=True),
        lax.all_gather(up_share, "gx", axis=0, tiled=True),
    )
    input_grad = lax.psum_scatter(
        contract_last(gate_delta, gate_weight) + contract_last(up_delta, up_weight),
        "gy",
        scatter_dimension=0,
        tiled=True,
    ).astype(jnp.bfloat16)
    gate_grad = contract_first(features, gate_delta).astype(jnp.bfloat16)
    up_grad = contract_first(features, up_delta).astype(jnp.bfloat16)
    down_grad = contract_first(hidden, grad_rows).astype(jnp.bfloat16)
    return (output, input_grad, gate_grad, up_grad, down_grad)


def solution(mesh):
    placed = (P("gy", "gx"), P("gx", "gy"), P("gx", "gy"), P("gy", "gx"), P("gy", "gx"))
    return jax.shard_map(
        shards,
        mesh=mesh,
        in_specs=placed,
        out_specs=(P("gy", "gx"), P("gy", "gx"), P("gx", "gy"), P("gx", "gy"), P("gy", "gx")),
        check_vma=False,
    )
```

profile of v0, /device:TPU:1, one launch (start us, length us, event | category | flops | bytes accessed | tf_op | source)
XLA Modules:
  0.0 579.7 jit_solution(1692257796891790483)
XLA Ops:
  7.2 0.0 copy-start
  7.2 0.0 copy-start.1
  7.2 0.0 all-reduce.5.cloned.1.call-start
  7.2 35.6 %all_gather.15 = bf16[256,576]{1,0:T(8,128)(2,1)S(1)} all-gather(bf16[16,576]{1,0:T(8,128)(2,1)} %param.5), channel_id=1, replica_groups=mesh['gx'=32,'gy'=16] {'gy'}, dimensions={0}, use_global_device_ids=true | all-gather | bytes 313344 | tf_op jit(solution)/shard_map/all_gather | solution.py:37
  42.8 0.0 copy-done
  42.8 0.5 fusion.3
  43.3 0.0 copy-done.1
  43.3 0.0 copy-start.5
  43.3 0.5 fusion.4
  43.8 0.3 copy-done.5
  44.0 24.3 %all_gather.17 = bf16[256,576]{1,0:T(8,128)(2,1)S(1)} all-gather(bf16[16,576]{1,0:T(8,128)(2,1)S(1)} %copy-done.5), channel_id=1, replica_groups=mesh['gx'=32,'gy'=16] {'gy'}, dimensions={0}, use_global_device_ids=true | all-gather | bytes 313344 | tf_op jit(solution)/shard_map/all_gather | solution.py:38
  68.3 0.0 copy-start.2
  68.3 1.1 pad_maximum_fusion
  69.4 0.3 copy-done.2
  69.7 1.2 fusion.6
  71.0 0.0 all-reduce.5.cloned.1.call-update
  71.0 0.0 reduce-scatter.7.cloned.1.call-start
  71.1 1.3 dynamic-slice
  73.0 281.8 %all-reduce.5.cloned.1.call-done = (f32[256,1152]{0,1:T(8,128)}, f32[256,576]{0,1:T(8,128)}) async-done(((f32[256,1152]{0,1:T(8,128)}, f32[256,576]{0,1:T(8,128)}), (f32[256,1152]{0,1:T(8,128)}, f32[256,576]{0,1:T(8,128)})) %all-reduce.5.cloned.1.call-update) | async-done | bytes 1769488
  354.7 2.1 constant_dynamic-slice_fusion
  356.9 1.1 copy.25
  357.9 0.1 copy.34
  358.1 0.1 copy.35
  358.3 42.6 %all_gather.18 = bf16[256,576]{1,0:T(8,128)(2,1)S(1)} all-gather(bf16[8,576]{1,0:T(8,128)(2,1)S(1)} %get-tuple-element.25), channel_id=1, replica_groups=mesh['gx'=32,'gy'=16] {'gx'}, dimensions={0}, use_global_device_ids=true | all-gather | bytes 304128 | tf_op jit(solution)/shard_map/all_gather | solution.py:64
  400.8 0.5 fusion.7
  401.3 38.8 %all_gather.19 = bf16[256,576]{1,0:T(8,128)(2,1)S(1)} all-gather(bf16[8,576]{1,0:T(8,128)(2,1)S(1)} %get-tuple-element.24), channel_id=1, replica_groups=mesh['gx'=32,'gy'=16] {'gx'}, dimensions={0}, use_global_device_ids=true | all-gather | bytes 304128 | tf_op jit(solution)/shard_map/all_gather | solution.py:65
  440.1 1.3 convolution_add_fusion
  441.4 0.0 reduce-scatter.7.cloned.1.call-update
  441.5 0.0 reduce-scatter.5.cloned.1.call-start
  441.5 37.8 %all_gather.16 = bf16[256,576]{1,0:T(8,128)(2,1)S(1)} all-gather(bf16[8,576]{1,0:T(8,128)(2,1)S(1)} %get-tuple-element.26), channel_id=1, replica_groups=mesh['gx'=32,'gy'=16] {'gx'}, dimensions={0}, use_global_device_ids=true | all-gather | bytes 304128 | tf_op jit(solution)/shard_map/all_gather | solution.py:50
  479.3 0.0 copy-start.3
  479.3 1.3 fusion.5
  480.6 0.0 copy-done.3
  480.7 0.0 reduce-scatter.5.cloned.1.call-update
  480.7 0.4 fusion
  481.1 1.2 copy.27
  482.3 0.0 copy-start.4
  482.3 0.4 fusion.1
  482.7 1.2 copy.28
  483.9 0.0 copy-done.4
  483.9 1.3 convolution_convert_fusion
  485.2 14.2 %reduce-scatter.7.cloned.1.call-done = f32[16,576]{1,0:T(8,128)} async-done(((f32[256,576]{1,0:T(8,128)}), f32[16,576]{1,0:T(8,128)}) %reduce-scatter.7.cloned.1.call-update) | async-done | bytes 36880 | tf_op jit(solution)/shard_map/reduce_scatter | solution.py:67
  499.3 1.4 convert_element_type.34
  500.7 71.0 %reduce-scatter.5.cloned.1.call-done = f32[16,576]{1,0:T(8,128)} async-done(((f32[256,576]{1,0:T(8,128)}), f32[16,576]{1,0:T(8,128)}) %reduce-scatter.5.cloned.1.call-update) | async-done | bytes 36880 | tf_op jit(solution)/shard_map/reduce_scatter | solution.py:52
  571.8 1.4 convert_element_type.31
  (1 shorter events, 0.0 us)
Async XLA Ops:
  7.2 35.7 %copy-start = (bf16[576,576]{1,0:T(8,128)(2,1)S(1)}, bf16[576,576]{1,0:T(8,128)(2,1)}, u32[]{:S(2)}) copy-start(bf16[576,576]{1,0:T(8,128)(2,1)} %param.6) | copy-start | bytes 1990660
  7.2 36.1 %copy-start.1 = (bf16[576,576]{1,0:T(8,128)(2,1)S(1)}, bf16[576,576]{1,0:T(8,128)(2,1)}, u32[]{:S(2)}) copy-start(bf16[576,576]{1,0:T(8,128)(2,1)} %param.7) | copy-start | bytes 1990660
  7.2 347.6 %all-reduce.5.cloned.1.call-start = ((), (), s32[]{:S(2)}) async-start(), calls=%async_computation.4 | async-start | bytes 3538944
  43.3 0.7 copy-start.5
  68.3 1.4 copy-start.2
  71.0 428.3 %reduce-scatter.7.cloned.1.call-start = ((), (), s32[]{:S(2)}) async-start(), calls=%async_computation.3 | async-start | bytes 696320 | tf_op jit(solution)/shard_map/reduce_scatter | solution.py:67
  441.5 130.3 %reduce-scatter.5.cloned.1.call-start = ((), (), s32[]{:S(2)}) async-start(), calls=%async_computation.2 | async-start | bytes 696320 | tf_op jit(solution)/shard_map/reduce_scatter | solution.py:52
  479.3 1.3 copy-start.3
  482.3 1.6 copy-start.4
Sparse Core Ops, SparseCore 0:
  71.1 283.5 all-reduce.4
  441.6 57.7 reduce-scatter.6
  502.1 69.5 reduce-scatter.4
where the time goes:
time: 591 us; the launch traced here: 580 us
  waiting for transfers between devices  367 us (62%)
  blocking collectives  179 us (30%)
  between operations  14.5 us (2%)
  local copies, waits for them, and re-layouts  7.67 us (1%)
  matrix products  7.37 us (1%)
    unnamed x4, waiting for transfers between devices  282 us
    reduce_scatter x1, waiting for transfers between devices, shards(): lax.psum_scatter(jnp.dot(block, down_weight, preferred_element_type=jnp.f...  71 us
    all_gather x1, blocking collectives, shards(): lax.all_gather(gate_share, 'gx', axis=0, tiled=True)  42.6 us
    all_gather x1, blocking collectives, shards(): lax.all_gather(up_share, 'gx', axis=0, tiled=True)  38.8 us
    all_gather x1, blocking collectives, shards(): hidden = lax.all_gather(hidden_share, 'gx', axis=0, tiled=True)  37.8 us
    all_gather x1, blocking collectives, shards(): lax.all_gather(tokens, 'gy', axis=0, tiled=True)  35.6 us
    all_gather x1, blocking collectives, shards(): lax.all_gather(cotangent, 'gy', axis=0, tiled=True)  24.3 us
    reduce_scatter x1, waiting for transfers between devices, shards(): lax.psum_scatter(contract_last(gate_delta, gate_weight) + contract_last(u...  14.2 us
  transfers between devices with their start and end apart: 3, of which 3 were waited for; matrix products, arithmetic and copies ran while one was open for 1% of the time, Pallas kernels for 0%

commit v1 on v0

v1 whole, which is shorter than its diff:
```python
import jax
import jax.numpy as jnp
from jax import lax
from jax.experimental import pallas as pl
from jax.experimental.pallas import tpu as pltpu
from jax.sharding import PartitionSpec as P

MESH = pl.DeviceIdType.MESH
F32 = jnp.float32
BF16 = jnp.bfloat16


def mm(a, b):
    return lax.dot_general(a, b, (((1,), (0,)), ((), ())), preferred_element_type=F32)


def mm_nt(a, b):
    return lax.dot_general(a, b, (((1,), (1,)), ((), ())), preferred_element_type=F32)


def mm_tn(a, b):
    return lax.dot_general(a, b, (((0,), (0,)), ((), ())), preferred_element_type=F32)


def each(start, stop, body):
    def step(i, carry):
        body(i)
        return carry

    lax.fori_loop(start, stop, step, 0)


def kernel(
    tok, wg, wu, wd, cot,
    out, ig, gate_grad, up_grad, down_grad,
    mine, w, xt, xc, xw, part, sgu, shg, rgu, rhg, gh, gd, ghp, gdp, so, si, ro, ri,
    lsem, wss, wrs, tss, trs, css, crs, guss, gurs, hgss, hgrs, hss, hrs, dss, drs,
    oss, ors, iss, irs, fss, frs,
):
    gx, gy = lax.axis_index("gx"), lax.axis_index("gy")
    q, c = lax.div(gx, 2), lax.rem(gx, 2)
    xh, y = lax.div(q, 8), lax.rem(q, 8)
    xl, z = lax.div(gy, 8), lax.rem(gy, 8)
    other = 1 - c
    peer = (q * 2 + other, gy)

    def row_chip(i):
        t = lax.rem(xh + lax.div(i, 8), 2) * 8 + lax.rem(y + i, 8)
        return t, (t * 2 + c, gy)

    def col_dev(i, core):
        return (q * 2 + core, lax.rem(xl + lax.div(i, 8), 2) * 8 + lax.rem(z + i, 8))

    def remote(src, dst, ssem, rsem, dev):
        return pltpu.make_async_remote_copy(
            src_ref=src, dst_ref=dst, send_sem=ssem, recv_sem=rsem, device_id=dev, device_id_type=MESH
        )

    loads = [
        pltpu.make_async_copy(src, dst, lsem.at[n])
        for n, (src, dst) in enumerate(
            [
                (tok, mine.at[0]), (cot, mine.at[1]),
                (wg, w.at[c, 0]), (wu, w.at[c, 1]), (wd, w.at[c, 2]),
            ]
        )
    ]
    for copy in loads:
        copy.start()

    barrier = pltpu.get_barrier_semaphore()

    def greet(dev):
        pl.semaphore_signal(barrier, inc=1, device_id=dev, device_id_type=MESH)

    each(1, 16, lambda i: greet(row_chip(i)[1]))

    def greet_col(i):
        greet(col_dev(i, xl))

        @pl.when(lax.rem(xl + lax.div(i, 8), 2) == c)
        def _():
            greet(col_dev(i, 1 - xl))

    each(1, 16, greet_col)
    greet(peer)
    pl.semaphore_wait(barrier, 15 + 15 + 8 - jnp.where(xl == c, 1, 0) + 1)

    loads[0].wait()
    loads[1].wait()

    def gather(n, dst, ss, rs):
        view = dst.at[c, pl.ds(pl.multiple_of(z * 16, 16), 16)]

        def desc(i):
            return remote(mine.at[n], view, ss.at[i], rs.at[c * 8 + z], col_dev(i, xl))

        def start():
            @pl.when(c == xl)
            def _():
                pltpu.make_async_copy(mine.at[n], view, rs.at[c * 8 + z]).start()

            @pl.when(c != xl)
            def _():
                desc(0).start()

            each(1, 16, lambda i: desc(i).start())

        def finish():
            @pl.when(c != xl)
            def _():
                desc(0).wait_send()

            each(1, 16, lambda i: desc(i).wait_send())

        def arrive():
            def one(s):
                rows = pl.ds(pl.multiple_of(lax.rem(s, 8) * 16, 16), 16)
                remote(mine.at[n], dst.at[lax.div(s, 8), rows], ss.at[0], rs.at[s], peer).wait_recv()

            each(0, 16, one)

        return start, finish, arrive

    tok_start, tok_finish, tok_arrive = gather(0, xt, tss, trs)
    cot_start, cot_finish, cot_arrive = gather(1, xc, css, crs)
    tok_start()
    wcopies = [
        remote(src, w.at[c, n], wss.at[n], wrs.at[n], peer) for n, src in enumerate((wg, wu, wd))
    ]
    for copy in wcopies:
        copy.start()
    cot_start()
    for copy in loads[2:]:
        copy.wait()
    wcopies[0].wait_recv()
    wcopies[1].wait_recv()

    def scatter(src, dst, ss, rs):
        def desc(i):
            t, dev = row_chip(i)
            return remote(src.at[t], dst.at[i], ss.at[i], rs.at[i], dev)

        return (
            lambda: each(1, 16, lambda i: desc(i).start()),
            lambda: each(1, 16, lambda i: desc(i).wait_send()),
            lambda: each(1, 16, lambda i: desc(i).wait_recv()),
        )

    gu_start, gu_finish, gu_arrive = scatter(sgu, rgu, guss, gurs)
    hg_start, hg_finish, hg_arrive = scatter(shg, rhg, hgss, hgrs)

    tok_arrive()
    for n in range(2):
        p = (mm(xt[0], w[0, n]) + mm(xt[1], w[1, n])).reshape(16, 8, 576)
        part[n] = p
        sgu[:, n] = p.astype(BF16)
    gu_start()
    wcopies[2].wait_recv()
    cot_arrive()
    p = (mm_nt(xc[0], w[0, 2]) + mm_nt(xc[1], w[1, 2])).reshape(16, 8, 576)
    part[2] = p
    shg[...] = p.astype(BF16)
    hg_start()

    fwd = [
        remote(xt.at[other], xw.at[0], fss.at[0], frs.at[0], peer),
        remote(xc.at[other], xw.at[1], fss.at[1], frs.at[1], peer),
        remote(gh, ghp, fss.at[2], frs.at[2], peer),
        remote(gd, gdp, fss.at[3], frs.at[3], peer),
    ]
    fwd[0].start()
    fwd[1].start()

    def spread(buf, ss, rs):
        def desc(i):
            return remote(buf.at[q], buf.at[q], ss.at[i], rs.at[i], row_chip(i)[1])

        return (
            lambda: each(1, 16, lambda i: desc(i).start()),
            lambda: each(1, 16, lambda i: desc(i).wait_send()),
            lambda: each(1, 16, lambda i: desc(i).wait_recv()),
        )

    h_start, h_finish, h_arrive = spread(gh, hss, hrs)
    d_start, d_finish, d_arrive = spread(gd, dss, drs)

    gu_arrive()
    gate, up = part[0, q], part[1, q]
    for i in range(1, 16):
        gate += rgu[i, 0].astype(F32)
        up += rgu[i, 1].astype(F32)
    sig = jax.nn.sigmoid(gate)
    act = gate * sig
    gh[q] = (act * up).astype(BF16)
    h_start()
    hg_arrive()
    hgrad = part[2, q]
    for i in range(1, 16):
        hgrad += rhg[i].astype(F32)
    gd[q, 0] = (hgrad * up * sig * (1.0 + gate * (1.0 - sig))).astype(BF16)
    gd[q, 1] = (hgrad * act).astype(BF16)
    d_start()

    def deliver(src, dst, ss, rs):
        slot = xl * 8 + z

        def dev_of(j):
            return (q * 2 + lax.div(j, 8), c * 8 + lax.rem(z + j, 8))

        def desc(j):
            rows = pl.ds(pl.multiple_of(lax.rem(z + j, 8) * 16, 16), 16)
            return remote(src.at[lax.div(j, 8), rows], dst.at[slot], ss.at[j], rs.at[slot], dev_of(j))

        def is_self(j):
            return (xl == c) & (j == c * 8)

        def start():
            def one(j):
                @pl.when(is_self(j))
                def _():
                    rows = pl.ds(pl.multiple_of(z * 16, 16), 16)
                    pltpu.make_async_copy(src.at[c, rows], dst.at[slot], rs.at[slot]).start()

                @pl.when(jnp.logical_not(is_self(j)))
                def _():
                    desc(j).start()

            each(0, 16, one)

        def finish():
            def one(j):
                @pl.when(jnp.logical_not(is_self(j)))
                def _():
                    desc(j).wait_send()

            each(0, 16, one)

        def arrive():
            def one(s):
                remote(src.at[0, pl.ds(0, 16)], dst.at[s], ss.at[0], rs.at[s], peer).wait_recv()

            each(0, 16, one)

        return start, finish, arrive

    o_start, o_finish, o_arrive = deliver(so, ro, oss, ors)
    i_start, i_finish, i_arrive = deliver(si, ri, iss, irs)

    h_arrive()
    fwd[2].start()
    hidden = gh[...].reshape(128, 576)
    for k in range(2):
        so[k] = mm(hidden, w[k, 2]).astype(BF16)
    o_start()
    fwd[0].wait_recv()
    fwd[1].wait_recv()
    fwd[2].wait_recv()
    down_grad[...] = (
        mm_tn(gh[...].reshape(128, 576), xc[c]) + mm_tn(ghp[...].reshape(128, 576), xw[1])
    ).astype(BF16)

    d_arrive()
    fwd[3].start()
    gdl, udl = gd[:, 0].reshape(128, 576), gd[:, 1].reshape(128, 576)
    for k in range(2):
        si[k] = (mm_nt(gdl, w[k, 0]) + mm_nt(udl, w[k, 1])).astype(BF16)
    i_start()
    fwd[3].wait_recv()
    for n, ref in enumerate((gate_grad, up_grad)):
        ref[...] = (
            mm_tn(xt[c], gd[:, n].reshape(128, 576)) + mm_tn(xw[0], gdp[:, n].reshape(128, 576))
        ).astype(BF16)

    def total(ref):
        t = ref[0].astype(F32)
        for s in range(1, 16):
            t += ref[s].astype(F32)
        return t.astype(BF16)

    o_arrive()
    out[...] = total(ro)
    i_arrive()
    ig[...] = total(ri)

    for copy in wcopies + fwd:
        copy.wait_send()
    for finish in (
        tok_finish, cot_finish, gu_finish, hg_finish, h_finish, d_finish, o_finish, i_finish
    ):
        finish()


def shards(tokens, gate_weight, up_weight, down_weight, cotangent):
    vmem = pl.BlockSpec(memory_space=pltpu.VMEM)
    hbm = pl.BlockSpec(memory_space=pl.ANY)
    dma = pltpu.SemaphoreType.DMA
    act = jax.ShapeDtypeStruct((16, 576), BF16)
    weight = jax.ShapeDtypeStruct((576, 576), BF16)
    return pl.pallas_call(
        kernel,
        out_shape=(act, act, weight, weight, weight),
        in_specs=[hbm] * 5,
        out_specs=(vmem,) * 5,
        scratch_shapes=[
            pltpu.VMEM((2, 16, 576), BF16),
            pltpu.VMEM((2, 3, 576, 576), BF16),
            pltpu.VMEM((2, 128, 576), BF16),
            pltpu.VMEM((2, 128, 576), BF16),
            pltpu.VMEM((2, 128, 576), BF16),
            pltpu.VMEM((3, 16, 8, 576), F32),
            pltpu.VMEM((16, 2, 8, 576), BF16),
            pltpu.VMEM((16, 8, 576), BF16),
            pltpu.VMEM((16, 2, 8, 576), BF16),
            pltpu.VMEM((16, 8, 576), BF16),
            pltpu.VMEM((16, 8, 576), BF16),
            pltpu.VMEM((16, 2, 8, 576), BF16),
            pltpu.VMEM((16, 8, 576), BF16),
            pltpu.VMEM((16, 2, 8, 576), BF16),
            pltpu.VMEM((2, 128, 576), BF16),
            pltpu.VMEM((2, 128, 576), BF16),
            pltpu.VMEM((16, 16, 576), BF16),
            pltpu.VMEM((16, 16, 576), BF16),
            dma((5,)),
            dma((3,)), dma((3,)),
        ]
        + [dma((16,))] * 16
        + [dma((4,))] * 2,
        compiler_params=pltpu.CompilerParams(
            collective_id=0, has_side_effects=True, vmem_limit_bytes=40 * 1024 * 1024
        ),
        cost_estimate=pl.CostEstimate(
            flops=9 * 2 * 256 * 576 * 576, bytes_accessed=6 * 576 * 576 * 2, transcendentals=8 * 576
        ),
    )(tokens, gate_weight, up_weight, down_weight, cotangent)


def solution(mesh):
    placed = (P("gy", "gx"), P("gx", "gy"), P("gx", "gy"), P("gy", "gx"), P("gy", "gx"))
    return jax.shard_map(
        shards,
        mesh=mesh,
        in_specs=placed,
        out_specs=(P("gy", "gx"), P("gy", "gx"), P("gx", "gy"), P("gx", "gy"), P("gy", "gx")),
        check_vma=False,
    )
```

time: 591 us -> 77.6 us (0.13); the launches traced: 580 us -> 77.2 us
  waiting for transfers between devices: 367 us -> 0 us
  blocking collectives: 179 us -> 0 us
  Pallas kernels: 0 us -> 68 us
  between operations: 14.5 us -> 0.66 us
  matrix products: 7.37 us -> 0 us
    unnamed x4 -> x0, waiting for transfers between devices: 282 us -> none
    all_gather x5 -> x0, blocking collectives: 179 us -> none  [the longest x1 42.6 us: shards(): lax.all_gather(gate_share, 'gx', axis=0, tiled=True)]
    reduce_scatter x2 -> x0, waiting for transfers between devices: 85.2 us -> none  [the longest x1 71 us: shards(): lax.psum_scatter(jnp.dot(block, down_weight, preferred_element_type=jnp.f...]
    pallas_call x0 -> x1, Pallas kernels: none -> 68 us  [shards(): pl.pallas_call(kernel, out_shape=(act, act, weight, weight, weight), in_s...]
    dot_general x9 -> x0, matrix products: 7.37 us -> none  [the longest x3 3.03 us: contract_last(): lax.dot_general(left, right, (((1,), (1,)), ((), ())), preferred_element_...]
  transfers between devices with their start and end apart: 3 -> 0, of which waited for: 3 -> 0; matrix products, arithmetic and copies ran while one was open for 1% -> 0% of each run, Pallas kernels for 0% -> 0%
where the time goes in v1:
time: 77.6 us; the launch traced here: 77.2 us
  Pallas kernels  68 us (88%)
  local copies, waits for them, and re-layouts  8.6 us (11%)
    pallas_call x1, Pallas kernels, shards(): pl.pallas_call(kernel, out_shape=(act, act, weight, weight, weight), in_s...  68 us
    unnamed x15, local copies, waits for them, and re-layouts  8.6 us

profile of v1, /device:TPU:1, one launch (start us, length us, event | category | flops | bytes accessed | tf_op | source)
XLA Modules:
  0.0 77.2 jit_solution(2112296649588671758)
XLA Ops:
  0.6 0.0 copy-start
  0.6 1.1 %copy-done = bf16[576,576]{1,0:T(8,128)(2,1)S(1)} copy-done((bf16[576,576]{1,0:T(8,128)(2,1)S(1)}, bf16[576,576]{1,0:T(8,128)(2,1)}, u32[]{:S(2)}) %copy-start) | copy-done | bytes 663576
  1.7 0.0 copy-start.1
  1.8 1.1 %copy-done.1 = bf16[576,576]{1,0:T(8,128)(2,1)S(1)} copy-done((bf16[576,576]{1,0:T(8,128)(2,1)S(1)}, bf16[576,576]{1,0:T(8,128)(2,1)}, u32[]{:S(2)}) %copy-start.1) | copy-done | bytes 663576
  2.9 0.0 copy-start.2
  2.9 1.1 %copy-done.2 = bf16[576,576]{1,0:T(8,128)(2,1)S(1)} copy-done((bf16[576,576]{1,0:T(8,128)(2,1)S(1)}, bf16[576,576]{1,0:T(8,128)(2,1)}, u32[]{:S(2)}) %copy-start.2) | copy-done | bytes 663576
  4.0 0.0 copy-start.3
  4.0 0.7 copy-done.3
  4.7 0.0 copy-start.4
  4.7 0.7 copy-done.4
  5.4 68.0 %shard_map.92 = (bf16[16,576]{1,0:T(8,128)(2,1)S(1)}, bf16[16,576]{1,0:T(8,128)(2,1)S(1)}, bf16[576,576]{1,0:T(8,128)(2,1)S(1)}, bf16[576,576]{1,0:T(8,128)(2,1)S(1)}, bf16[576,576]{1,0:T(8,128)(2,1)S(1)}) custom-call(bf16[16,576]{1,0:T(8,128)(2,1)S(1)} %copy-done.3, bf16[576,576]{1,0:T(8,128)(2,1)S(1)} %copy-done, bf16[576,576]{1,0:T(8,128)(2,1)S(1)} %copy-done.1, ...), custom_call_target="tpu_custom_call" | custom-call | flops 1528823808 | bytes 3981312 | tf_op jit(solution)/shard_map/pallas_call | solution.py:300
  73.4 0.6 copy.15
  74.0 0.6 copy.16
  74.7 0.9 %copy.17 = bf16[576,576]{1,0:T(8,128)(2,1)} copy(bf16[576,576]{1,0:T(8,128)(2,1)S(1)} %get-tuple-element.12) | data formatting | bytes 1327104
  75.5 0.9 %copy.18 = bf16[576,576]{1,0:T(8,128)(2,1)} copy(bf16[576,576]{1,0:T(8,128)(2,1)S(1)} %get-tuple-element.13) | data formatting | bytes 1327104
  76.4 0.9 %copy.19 = bf16[576,576]{1,0:T(8,128)(2,1)} copy(bf16[576,576]{1,0:T(8,128)(2,1)S(1)} %get-tuple-element.14) | data formatting | bytes 1327104
Async XLA Ops:
  0.6 1.1 %copy-start = (bf16[576,576]{1,0:T(8,128)(2,1)S(1)}, bf16[576,576]{1,0:T(8,128)(2,1)}, u32[]{:S(2)}) copy-start(bf16[576,576]{1,0:T(8,128)(2,1)} %wg.1) | copy-start | bytes 1990660
  1.7 1.1 %copy-start.1 = (bf16[576,576]{1,0:T(8,128)(2,1)S(1)}, bf16[576,576]{1,0:T(8,128)(2,1)}, u32[]{:S(2)}) copy-start(bf16[576,576]{1,0:T(8,128)(2,1)} %wu.1) | copy-start | bytes 1990660
  2.9 1.1 %copy-start.2 = (bf16[576,576]{1,0:T(8,128)(2,1)S(1)}, bf16[576,576]{1,0:T(8,128)(2,1)}, u32[]{:S(2)}) copy-start(bf16[576,576]{1,0:T(8,128)(2,1)} %wd.1) | copy-start | bytes 1990660
  4.0 0.7 copy-start.3
  4.7 0.7 copy-start.4

commit v2 on v1

v2 whole, which is shorter than its diff:
```python
import jax
import jax.numpy as jnp
from jax import lax
from jax.experimental import pallas as pl
from jax.experimental.pallas import tpu as pltpu
from jax.sharding import PartitionSpec as P

MESH = pl.DeviceIdType.MESH
F32 = jnp.float32
BF16 = jnp.bfloat16


def mm(a, b):
    return lax.dot_general(a, b, (((1,), (0,)), ((), ())), preferred_element_type=F32)


def mm_tn(a, b):
    return lax.dot_general(a, b, (((0,), (0,)), ((), ())), preferred_element_type=F32)


def each(start, stop, body):
    def step(i, carry):
        body(i)
        return carry

    lax.fori_loop(start, stop, step, 0)


def kernel(
    tok, wg, wu, wd, cot,
    out, ig, gate_grad, up_grad, down_grad,
    mine, packed, w, wj, wt, wdt, xt, xc, xw, pgu, phg, sgu, shg, rgu, rhg, gh, gd, ghp, gdp, so, si, ro, ri, act_out, w_out,
    near, lsem, wsem, wss, wrs, tss, trs, css, crs, guss, gurs, hgss, hgrs, hss, hrs, dss, drs,
    oss, ors, iss, irs, fss, frs,
):
    gx, gy = lax.axis_index("gx"), lax.axis_index("gy")
    c = lax.rem(gx, 2)
    xh, y = lax.div(gx, 16), lax.rem(lax.div(gx, 2), 8)
    xl, z = lax.div(gy, 8), lax.rem(gy, 8)
    other = 1 - c
    me = y * 2 + xh

    def row_dev(dx, dy):
        return (lax.rem(xh + dx, 2) * 16 + lax.rem(y + dy + 8, 8) * 2 + c, gy)

    def col_dev(dx, dz, core):
        return (gx - c + core, lax.rem(xl + dx, 2) * 8 + lax.rem(z + dz + 8, 8))

    peer = col_dev(0, 0, other)

    def remote(src, dst, ssem, rsem, dev):
        return pltpu.make_async_remote_copy(
            src_ref=src, dst_ref=dst, send_sem=ssem, recv_sem=rsem, device_id=dev, device_id_type=MESH
        )

    loads = [
        pltpu.make_async_copy(src, dst, lsem.at[n])
        for n, (src, dst) in enumerate(
            [
                (tok, mine.at[0]), (cot, mine.at[1]),
                (wg, w.at[c, 0]), (wu, w.at[c, 1]), (wd, w.at[c, 2]),
            ]
        )
    ]
    for copy in loads:
        copy.start()

    def greet(sem):
        def one(i):
            dx, d = lax.div(i, 5), lax.rem(i, 5) - 2

            @pl.when(i != 2)
            def _():
                pl.semaphore_signal(sem, inc=1, device_id=row_dev(dx, d), device_id_type=MESH)
                pl.semaphore_signal(sem, inc=1, device_id=col_dev(dx, d, c), device_id_type=MESH)

            pl.semaphore_signal(sem, inc=1, device_id=col_dev(dx, d, other), device_id_type=MESH)

        each(0, 10, one)

    barrier = pltpu.get_barrier_semaphore()
    greet(barrier)
    pl.semaphore_wait(barrier, 28)

    loads[0].wait()
    loads[1].wait()
    for n in range(2):
        packed[n] = jnp.concatenate([mine[n, :8], mine[n, 8:]], axis=1)

    def gather(n, dst, ss, rs):
        slot = z * 2 + c

        def desc(i):
            dx, d = lax.div(i, 5), lax.rem(i, 5) - 2
            return remote(packed.at[n], dst.at[z, c], ss.at[i], rs.at[slot], col_dev(dx, d, xl))

        def local():
            return pltpu.make_async_copy(packed.at[n], dst.at[z, c], rs.at[slot])

        def start():
            @pl.when(c == xl)
            def _():
                local().start()

            def one(i):
                @pl.when((i != 2) | (c != xl))
                def _():
                    desc(i).start()

            each(0, 10, one)

        def ahead(side):
            zs = lax.rem(z - 2 * side + 8, 8)
            k = (1 - side) // 2
            third = remote(dst.at[zs], dst.at[zs], ss.at[10 + k], rs.at[16 + k], col_dev(0, side, c))
            fourth = remote(
                dst.at[zs, k], dst.at[zs, k], ss.at[12 + k], rs.at[18 + k], col_dev(0, 2 * side, c)
            )
            return zs, third, fourth

        def here(zs, k):
            remote(packed.at[n], dst.at[zs, k], ss.at[0], rs.at[zs * 2 + k], peer).wait_recv()

        def forward():
            for side in (1, -1):
                zs, third, fourth = ahead(side)
                here(zs, 0)
                here(zs, 1)
                third.start()
                fourth.start()

        def arrive():
            for d in (0, 1, -1):
                zs = lax.rem(z + d + 8, 8)
                here(zs, 0)
                here(zs, 1)
            for side in (1, -1):
                _, third, fourth = ahead(side)
                third.wait_recv()
                fourth.wait_recv()

        def finish():
            def one(i):
                @pl.when((i != 2) | (c != xl))
                def _():
                    desc(i).wait_send()

            each(0, 10, one)
            for side in (1, -1):
                _, third, fourth = ahead(side)
                third.wait_send()
                fourth.wait_send()

        return start, forward, arrive, finish

    tok_start, tok_forward, tok_arrive, tok_finish = gather(0, xt, tss, trs)
    cot_start, cot_forward, cot_arrive, cot_finish = gather(1, xc, css, crs)
    tok_start()
    cot_start()
    wcopies = [
        remote(src, w.at[c, n], wss.at[n], wrs.at[n], peer) for n, src in enumerate((wg, wu, wd))
    ]
    for copy in wcopies:
        copy.start()
    greet(near)
    tok_forward()
    cot_forward()
    for copy in loads[2:]:
        copy.wait()
    wcopies[0].wait_recv()
    wcopies[1].wait_recv()
    for k in range(2):
        wj[k] = jnp.concatenate([w[k, 0], w[k, 1]], axis=1)
    pl.semaphore_wait(near, 28)
    wcopies[2].wait_recv()
    for k in range(2):
        wdt[k] = w[k, 2].T
        wt[k] = jnp.concatenate([w[k, 0].T, w[k, 1].T], axis=0)

    def rows(x):
        x = x.reshape(64, 1152)
        return jnp.concatenate([x[:, :576], x[:, 576:]], axis=0)

    def shares(x):
        return jnp.concatenate([x[:64], x[64:]], axis=1).reshape(8, 8, 1152)

    def scatter(src, dst, ss, rs):
        def desc(i):
            dx, dy = lax.rem(i, 2), lax.div(i, 2)
            t = lax.rem(y + dy, 8) * 2 + lax.rem(xh + dx, 2)
            return remote(src.at[t], dst.at[i], ss.at[i], rs.at[i], row_dev(dx, dy))

        return (
            lambda: each(1, 16, lambda i: desc(i).start()),
            lambda: each(1, 16, lambda i: desc(i).wait_recv()),
            lambda: each(1, 16, lambda i: desc(i).wait_send()),
        )

    gu_start, gu_arrive, gu_finish = scatter(sgu, rgu, guss, gurs)
    hg_start, hg_arrive, hg_finish = scatter(shg, rhg, hgss, hgrs)

    tok_arrive()
    p = mm(rows(xt[:, 0]), wj[0]) + mm(rows(xt[:, 1]), wj[1])
    sgu[...] = p.reshape(16, 8, 1152).astype(BF16)
    gu_start()
    pgu[...] = p.reshape(16, 8, 1152)
    cot_arrive()
    p = mm(rows(xc[:, 0]), wdt[0]) + mm(rows(xc[:, 1]), wdt[1])
    shg[...] = p.reshape(16, 8, 576).astype(BF16)
    hg_start()
    phg[...] = p.reshape(16, 8, 576)

    fwd = [
        remote(xt.at[:, other], xw.at[0], fss.at[0], frs.at[0], peer),
        remote(xc.at[:, other], xw.at[1], fss.at[1], frs.at[1], peer),
        remote(gh, ghp, fss.at[2], frs.at[2], peer),
        remote(gd, gdp, fss.at[3], frs.at[3], peer),
    ]
    fwd[0].start()
    fwd[1].start()

    def spread(buf, ss, rs):
        def desc(i):
            return remote(
                buf.at[me], buf.at[me], ss.at[i], rs.at[me], row_dev(lax.div(i, 5), lax.rem(i, 5) - 2)
            )

        def near_one(i):
            @pl.when(i != 2)
            def _():
                desc(i).start()

        def pair(dy):
            return pl.ds(pl.multiple_of(lax.rem(y + dy + 8, 8) * 2, 2), 2)

        def here(dy):
            ys = lax.rem(y + dy + 8, 8)
            for k in range(2):
                remote(buf.at[me], buf.at[ys * 2 + k], ss.at[0], rs.at[ys * 2 + k], peer).wait_recv()

        def third(side):
            view = buf.at[pair(-2 * side)]
            k = (1 - side) // 2
            return remote(view, view, ss.at[10 + k], rs.at[16 + k], row_dev(0, side))

        def fourth():
            side = 1 - 2 * c
            view = buf.at[pair(-2 * side)]
            return remote(view, view, ss.at[12], rs.at[18], row_dev(0, 2 * side))

        def forward():
            for side in (1, -1):
                here(-2 * side)
                third(side).start()
            fourth().start()

        def arrive():
            remote(buf.at[me], buf.at[me], ss.at[0], rs.at[y * 2 + 1 - xh], peer).wait_recv()
            here(1)
            here(-1)
            third(1).wait_recv()
            third(-1).wait_recv()
            fourth().wait_recv()

        def finish():
            def one(i):
                @pl.when(i != 2)
                def _():
                    desc(i).wait_send()

            each(0, 10, one)
            third(1).wait_send()
            third(-1).wait_send()
            fourth().wait_send()

        return lambda: each(0, 10, near_one), forward, arrive, finish

    h_start, h_forward, h_arrive, h_finish = spread(gh, hss, hrs)
    d_start, d_forward, d_arrive, d_finish = spread(gd, dss, drs)

    gu_arrive()
    total = pgu[me]
    for i in range(1, 16):
        total += rgu[i].astype(F32)
    gate, up = total[:, :576], total[:, 576:]
    sig = jax.nn.sigmoid(gate)
    act = gate * sig
    gh[me] = (act * up).astype(BF16)
    h_start()
    slope = up * sig * (1.0 + gate * (1.0 - sig))
    both = jnp.concatenate([slope, act], axis=1)
    hg_arrive()
    hgrad = phg[me]
    for i in range(1, 16):
        hgrad += rhg[i].astype(F32)
    gd[me] = (jnp.concatenate([hgrad, hgrad], axis=1) * both).astype(BF16)
    d_start()
    h_forward()
    d_forward()

    def deliver(src, dst, ss, rs):
        slot = xl * 8 + z

        def desc(k, j):
            zt = lax.rem(z + j, 8)
            return remote(
                src.at[k, zt], dst.at[slot], ss.at[k * 8 + j], rs.at[slot], (gx - c + k, c * 8 + zt)
            )

        def is_self(k, j):
            return (xl == c) & (c == k) & (j == 0)

        def start(k):
            def one(j):
                @pl.when(is_self(k, j))
                def _():
                    pltpu.make_async_copy(src.at[k, z], dst.at[slot], rs.at[slot]).start()

                @pl.when(jnp.logical_not(is_self(k, j)))
                def _():
                    desc(k, j).start()

            each(0, 8, one)

        def arrive():
            each(
                0, 16, lambda s: remote(src.at[0, 0], dst.at[s], ss.at[0], rs.at[s], peer).wait_recv()
            )

        def finish():
            for k in range(2):

                def one(j):
                    @pl.when(jnp.logical_not(is_self(k, j)))
                    def _():
                        desc(k, j).wait_send()

                each(0, 8, one)

        return start, arrive, finish

    o_start, o_arrive, o_finish = deliver(so, ro, oss, ors)
    i_start, i_arrive, i_finish = deliver(si, ri, iss, irs)

    h_arrive()
    fwd[2].start()
    hidden = gh[...].reshape(128, 576)
    for k in range(2):
        so[k] = shares(mm(hidden, w[k, 2])).astype(BF16)
        o_start(k)
    for copy in fwd[:3]:
        copy.wait_recv()

    def own(x):
        return rows(x[:, pl.ds(c, 1)])

    stores = [
        pltpu.make_async_copy(src, dst, wsem.at[n])
        for n, (src, dst) in enumerate(
            [
                (act_out.at[0], out), (act_out.at[1], ig),
                (w_out.at[0], gate_grad), (w_out.at[1], up_grad), (w_out.at[2], down_grad),
            ]
        )
    ]
    w_out[2] = (
        mm_tn(gh[...].reshape(128, 576), own(xc)) + mm_tn(ghp[...].reshape(128, 576), rows(xw[1]))
    ).astype(BF16)
    stores[4].start()

    d_arrive()
    fwd[3].start()
    joined = gd[...].reshape(128, 1152)
    for k in range(2):
        si[k] = shares(mm(joined, wt[k])).astype(BF16)
        i_start(k)
    fwd[3].wait_recv()
    both = mm_tn(own(xt), gd[...].reshape(128, 1152)) + mm_tn(
        rows(xw[0]), gdp[...].reshape(128, 1152)
    )
    w_out[0] = both[:, :576].astype(BF16)
    w_out[1] = both[:, 576:].astype(BF16)
    stores[2].start()
    stores[3].start()

    def summed(ref):
        t = ref[0].astype(F32)
        for s in range(1, 16):
            t += ref[s].astype(F32)
        return jnp.concatenate([t[:, :576], t[:, 576:]], axis=0).astype(BF16)

    o_arrive()
    act_out[0] = summed(ro)
    stores[0].start()
    for copy in wcopies + fwd:
        copy.wait_send()
    for finish in (tok_finish, cot_finish, gu_finish, hg_finish, h_finish, d_finish, o_finish):
        finish()
    i_arrive()
    act_out[1] = summed(ri)
    stores[1].start()
    i_finish()
    for copy in stores:
        copy.wait()


def write_back(*refs):
    ins, outs, bufs, get, put = refs[:5], refs[5:10], refs[10:15], refs[15], refs[16]
    parts = [(n, slice(None)) for n in range(2)]
    parts += [(n, pl.ds(r * 192, 192)) for r in range(3) for n in range(2, 5)]
    reads = [pltpu.make_async_copy(ins[n].at[r], bufs[n].at[r], get.at[i]) for i, (n, r) in enumerate(parts)]
    writes = [pltpu.make_async_copy(bufs[n].at[r], outs[n].at[r], put.at[i]) for i, (n, r) in enumerate(parts)]
    for copy in reads:
        copy.start()
    for read, write in zip(reads, writes):
        read.wait()
        write.start()
    for copy in writes:
        copy.wait()


def shards(tokens, gate_weight, up_weight, down_weight, cotangent):
    hbm = pl.BlockSpec(memory_space=pltpu.HBM)
    dma = pltpu.SemaphoreType.DMA
    act = jax.ShapeDtypeStruct((16, 576), BF16)
    weight = jax.ShapeDtypeStruct((576, 576), BF16)
    results = pl.pallas_call(
        kernel,
        out_shape=(act, act, weight, weight, weight),
        in_specs=[hbm] * 5,
        out_specs=(hbm,) * 5,
        scratch_shapes=[
            pltpu.VMEM((2, 16, 576), BF16),
            pltpu.VMEM((2, 8, 1152), BF16),
            pltpu.VMEM((2, 3, 576, 576), BF16),
            pltpu.VMEM((2, 576, 1152), BF16),
            pltpu.VMEM((2, 1152, 576), BF16),
            pltpu.VMEM((2, 576, 576), BF16),
            pltpu.VMEM((8, 2, 8, 1152), BF16),
            pltpu.VMEM((8, 2, 8, 1152), BF16),
            pltpu.VMEM((2, 8, 8, 1152), BF16),
            pltpu.VMEM((16, 8, 1152), F32),
            pltpu.VMEM((16, 8, 576), F32),
            pltpu.VMEM((16, 8, 1152), BF16),
            pltpu.VMEM((16, 8, 576), BF16),
            pltpu.VMEM((16, 8, 1152), BF16),
            pltpu.VMEM((16, 8, 576), BF16),
            pltpu.VMEM((16, 8, 576), BF16),
            pltpu.VMEM((16, 8, 1152), BF16),
            pltpu.VMEM((16, 8, 576), BF16),
            pltpu.VMEM((16, 8, 1152), BF16),
            pltpu.VMEM((2, 8, 8, 1152), BF16),
            pltpu.VMEM((2, 8, 8, 1152), BF16),
            pltpu.VMEM((16, 8, 1152), BF16),
            pltpu.VMEM((16, 8, 1152), BF16),
            pltpu.VMEM((2, 16, 576), BF16),
            pltpu.VMEM((3, 576, 576), BF16),
            pltpu.SemaphoreType.REGULAR,
            dma((5,)), dma((5,)),
            dma((3,)), dma((3,)),
            dma((14,)), dma((20,)), dma((14,)), dma((20,)),
            dma((16,)), dma((16,)), dma((16,)), dma((16,)),
            dma((13,)), dma((19,)), dma((13,)), dma((19,)),
            dma((16,)), dma((16,)), dma((16,)), dma((16,)),
            dma((4,)), dma((4,)),
        ],
        compiler_params=pltpu.CompilerParams(
            collective_id=0, has_side_effects=True, vmem_limit_bytes=64 * 1024 * 1024
        ),
        cost_estimate=pl.CostEstimate(
            flops=9 * 2 * 256 * 576 * 576, bytes_accessed=6 * 576 * 576 * 2, transcendentals=8 * 576
        ),
    )(tokens, gate_weight, up_weight, down_weight, cotangent)
    return pl.pallas_call(
        write_back,
        out_shape=(act, act, weight, weight, weight),
        in_specs=[hbm] * 5,
        out_specs=(hbm,) * 5,
        scratch_shapes=[pltpu.VMEM(t.shape, BF16) for t in (act, act, weight, weight, weight)]
        + [dma((11,)), dma((11,))],
        compiler_params=pltpu.CompilerParams(vmem_limit_bytes=64 * 1024 * 1024),
    )(*results)


def solution(mesh):
    placed = (P("gy", "gx"), P("gx", "gy"), P("gx", "gy"), P("gy", "gx"), P("gy", "gx"))
    return jax.shard_map(
        shards,
        mesh=mesh,
        in_specs=placed,
        out_specs=(P("gy", "gx"), P("gy", "gx"), P("gx", "gy"), P("gx", "gy"), P("gy", "gx")),
        check_vma=False,
    )
```

time: 77.6 us -> 68.8 us (0.89)
  local copies, waits for them, and re-layouts: 8.6 us -> 0 us
    unnamed x15 -> x0, local copies, waits for them, and re-layouts: 8.6 us -> none
    pallas_call x0 -> x1, Pallas kernels: none -> 2.59 us  [shards(): pl.pallas_call(write_back, out_shape=(act, act, weight, weight, weight),...]
    pallas_call x1, Pallas kernels: 68 us -> 65.4 us  [shards(): pl.pallas_call(kernel, out_shape=(act, act, weight, weight, weight), in_s...]
where the time goes in v2:
time: 68.8 us; the launch traced here: 68.7 us
  Pallas kernels  68 us (99%)
    pallas_call x1, Pallas kernels, shards(): pl.pallas_call(kernel, out_shape=(act, act, weight, weight, weight), in_s...  65.4 us
    pallas_call x1, Pallas kernels, shards(): pl.pallas_call(write_back, out_shape=(act, act, weight, weight, weight),...  2.59 us

profile of v2, /device:TPU:1, one launch (start us, length us, event | category | flops | bytes accessed | tf_op | source)
XLA Modules:
  0.0 68.7 jit_solution(112979519514679398)
XLA Ops:
  0.6 65.4 %shard_map.92 = (bf16[16,576]{1,0:T(8,128)(2,1)}, bf16[16,576]{1,0:T(8,128)(2,1)}, bf16[576,576]{1,0:T(8,128)(2,1)}, bf16[576,576]{1,0:T(8,128)(2,1)}, bf16[576,576]{1,0:T(8,128)(2,1)}) custom-call(bf16[16,576]{1,0:T(8,128)(2,1)} %tok.1, bf16[576,576]{1,0:T(8,128)(2,1)} %wg.1, bf16[576,576]{1,0:T(8,128)(2,1)} %wu.1, bf16[576,576]{1,0:T(8,128)(2,1)} %wd.1, ...), custom_call_target="tpu_custom_call" | custom-call | flops 1528823808 | bytes 3981312 | tf_op jit(solution)/shard_map/pallas_call | solution.py:427
  66.1 2.6 %shard_map.93 = (bf16[16,576]{1,0:T(8,128)(2,1)}, bf16[16,576]{1,0:T(8,128)(2,1)}, bf16[576,576]{1,0:T(8,128)(2,1)}, bf16[576,576]{1,0:T(8,128)(2,1)}, bf16[576,576]{1,0:T(8,128)(2,1)}) custom-call(bf16[16,576]{1,0:T(8,128)(2,1)} %get-tuple-element.10.refs_0_, bf16[16,576]{1,0:T(8,128)(2,1)} %get-tuple-element.11.refs_1_, ...), custom_call_target="tpu_custom_call" | custom-call | tf_op jit(solution)/shard_map/pallas_call | solution.py:474

commit v3 on v2

--- a/solution.py
+++ b/solution.py
@@ -29,22 +29,22 @@
 def kernel(
     tok, wg, wu, wd, cot,
     out, ig, gate_grad, up_grad, down_grad,
-    mine, packed, w, wj, wt, wdt, xt, xc, xw, pgu, phg, sgu, shg, rgu, rhg, gh, gd, ghp, gdp, so, si, ro, ri, act_out, w_out,
-    near, lsem, wsem, wss, wrs, tss, trs, css, crs, guss, gurs, hgss, hgrs, hss, hrs, dss, drs,
+    mine, packed, w, wj, wt, wdt, xt, xc, xw, pgu, phg, sgu, shg, rgu, rhg, gh, gd, ghp, gdp, so, si, ro, ri,
+    near, lsem, wss, wrs, tss, trs, css, crs, guss, gurs, hgss, hgrs, hss, hrs, dss, drs,
     oss, ors, iss, irs, fss, frs,
 ):
     gx, gy = lax.axis_index("gx"), lax.axis_index("gy")
-    c = lax.rem(gx, 2)
-    xh, y = lax.div(gx, 16), lax.rem(lax.div(gx, 2), 8)
-    xl, z = lax.div(gy, 8), lax.rem(gy, 8)
+    c = gx & 1
+    xh, y = gx >> 4, (gx >> 1) & 7
+    xl, z = gy >> 3, gy & 7
     other = 1 - c
     me = y * 2 + xh
 
     def row_dev(dx, dy):
-        return (lax.rem(xh + dx, 2) * 16 + lax.rem(y + dy + 8, 8) * 2 + c, gy)
+        return (((xh + dx) & 1) * 16 + ((y + dy) & 7) * 2 + c, gy)
 
     def col_dev(dx, dz, core):
-        return (gx - c + core, lax.rem(xl + dx, 2) * 8 + lax.rem(z + dz + 8, 8))
+        return (gx - c + core, ((xl + dx) & 1) * 8 + ((z + dz) & 7))
 
     peer = col_dev(0, 0, other)
 
@@ -52,6 +52,18 @@
         return pltpu.make_async_remote_copy(
             src_ref=src, dst_ref=dst, send_sem=ssem, recv_sem=rsem, device_id=dev, device_id_type=MESH
         )
+
+    def greet(sem):
+        for d in (2, -2, 1, -1, 0):
+            for dx in (1, 0):
+                devs = [col_dev(dx, d, other)]
+                if dx or d:
+                    devs += [row_dev(dx, d), col_dev(dx, d, c)]
+                for dev in devs:
+                    pl.semaphore_signal(sem, inc=1, device_id=dev, device_id_type=MESH)
+
+    barrier = pltpu.get_barrier_semaphore()
+    greet(barrier)
 
     loads = [
         pltpu.make_async_copy(src, dst, lsem.at[n])
@@ -65,21 +77,6 @@
     for copy in loads:
         copy.start()
 
-    def greet(sem):
-        def one(i):
-            dx, d = lax.div(i, 5), lax.rem(i, 5) - 2
-
-            @pl.when(i != 2)
-            def _():
-                pl.semaphore_signal(sem, inc=1, device_id=row_dev(dx, d), device_id_type=MESH)
-                pl.semaphore_signal(sem, inc=1, device_id=col_dev(dx, d, c), device_id_type=MESH)
-
-            pl.semaphore_signal(sem, inc=1, device_id=col_dev(dx, d, other), device_id_type=MESH)
-
-        each(0, 10, one)
-
-    barrier = pltpu.get_barrier_semaphore()
-    greet(barrier)
     pl.semaphore_wait(barrier, 28)
 
     loads[0].wait()
@@ -90,27 +87,29 @@
     def gather(n, dst, ss, rs):
         slot = z * 2 + c
 
+        places = [(dx, d) for d in (2, -2, 1, -1, 0) for dx in (1, 0)]
+
         def desc(i):
-            dx, d = lax.div(i, 5), lax.rem(i, 5) - 2
+            dx, d = places[i]
             return remote(packed.at[n], dst.at[z, c], ss.at[i], rs.at[slot], col_dev(dx, d, xl))
 
         def local():
             return pltpu.make_async_copy(packed.at[n], dst.at[z, c], rs.at[slot])
 
         def start():
+            for i in range(9):
+                desc(i).start()
+
             @pl.when(c == xl)
             def _():
                 local().start()
 
-            def one(i):
-                @pl.when((i != 2) | (c != xl))
-                def _():
-                    desc(i).start()
-
-            each(0, 10, one)
+            @pl.when(c != xl)
+            def _():
+                desc(9).start()
 
         def ahead(side):
-            zs = lax.rem(z - 2 * side + 8, 8)
+            zs = (z - 2 * side) & 7
             k = (1 - side) // 2
             third = remote(dst.at[zs], dst.at[zs], ss.at[10 + k], rs.at[16 + k], col_dev(0, side, c))
             fourth = remote(
@@ -131,7 +130,7 @@
 
         def arrive():
             for d in (0, 1, -1):
-                zs = lax.rem(z + d + 8, 8)
+                zs = (z + d) & 7
                 here(zs, 0)
                 here(zs, 1)
             for side in (1, -1):
@@ -140,12 +139,13 @@
                 fourth.wait_recv()
 
         def finish():
-            def one(i):
-                @pl.when((i != 2) | (c != xl))
-                def _():
-                    desc(i).wait_send()
-
-            each(0, 10, one)
+            for i in range(9):
+                desc(i).wait_send()
+
+            @pl.when(c != xl)
+            def _():
+                desc(9).wait_send()
+
             for side in (1, -1):
                 _, third, fourth = ahead(side)
                 third.wait_send()
@@ -156,7 +156,6 @@
     tok_start, tok_forward, tok_arrive, tok_finish = gather(0, xt, tss, trs)
     cot_start, cot_forward, cot_arrive, cot_finish = gather(1, xc, css, crs)
     tok_start()
-    cot_start()
     wcopies = [
         remote(src, w.at[c, n], wss.at[n], wrs.at[n], peer) for n, src in enumerate((wg, wu, wd))
     ]
@@ -164,7 +163,7 @@
         copy.start()
     greet(near)
     tok_forward()
-    cot_forward()
+    cot_start()
     for copy in loads[2:]:
         copy.wait()
     wcopies[0].wait_recv()
@@ -172,10 +171,6 @@
     for k in range(2):
         wj[k] = jnp.concatenate([w[k, 0], w[k, 1]], axis=1)
     pl.semaphore_wait(near, 28)
-    wcopies[2].wait_recv()
-    for k in range(2):
-        wdt[k] = w[k, 2].T
-        wt[k] = jnp.concatenate([w[k, 0].T, w[k, 1].T], axis=0)
 
     def rows(x):
         x = x.reshape(64, 1152)
@@ -186,8 +181,8 @@
 
     def scatter(src, dst, ss, rs):
         def desc(i):
-            dx, dy = lax.rem(i, 2), lax.div(i, 2)
-            t = lax.rem(y + dy, 8) * 2 + lax.rem(xh + dx, 2)
+            dx, dy = i & 1, i >> 1
+            t = ((y + dy) & 7) * 2 + ((xh + dx) & 1)
             return remote(src.at[t], dst.at[i], ss.at[i], rs.at[i], row_dev(dx, dy))
 
         return (
@@ -204,11 +199,17 @@
     sgu[...] = p.reshape(16, 8, 1152).astype(BF16)
     gu_start()
     pgu[...] = p.reshape(16, 8, 1152)
+    cot_forward()
+    wcopies[2].wait_recv()
+    for k in range(2):
+        wdt[k] = w[k, 2].T
     cot_arrive()
     p = mm(rows(xc[:, 0]), wdt[0]) + mm(rows(xc[:, 1]), wdt[1])
     shg[...] = p.reshape(16, 8, 576).astype(BF16)
     hg_start()
     phg[...] = p.reshape(16, 8, 576)
+    for k in range(2):
+        wt[k] = jnp.concatenate([w[k, 0].T, w[k, 1].T], axis=0)
 
     fwd = [
         remote(xt.at[:, other], xw.at[0], fss.at[0], frs.at[0], peer),
@@ -220,21 +221,20 @@
     fwd[1].start()
 
     def spread(buf, ss, rs):
+        places = [(dx, d) for d in (2, -2, 1, -1, 0) for dx in (1, 0)]
+
         def desc(i):
-            return remote(
-                buf.at[me], buf.at[me], ss.at[i], rs.at[me], row_dev(lax.div(i, 5), lax.rem(i, 5) - 2)
-            )
-
-        def near_one(i):
-            @pl.when(i != 2)
-            def _():
+            return remote(buf.at[me], buf.at[me], ss.at[i], rs.at[me], row_dev(*places[i]))
+
+        def start():
+            for i in range(9):
                 desc(i).start()
 
         def pair(dy):
-            return pl.ds(pl.multiple_of(lax.rem(y + dy + 8, 8) * 2, 2), 2)
+            return pl.ds(pl.multiple_of(((y + dy) & 7) * 2, 2), 2)
 
         def here(dy):
-            ys = lax.rem(y + dy + 8, 8)
+            ys = (y + dy) & 7
             for k in range(2):
                 remote(buf.at[me], buf.at[ys * 2 + k], ss.at[0], rs.at[ys * 2 + k], peer).wait_recv()
 
@@ -263,17 +263,13 @@
             fourth().wait_recv()
 
         def finish():
-            def one(i):
-                @pl.when(i != 2)
-                def _():
-                    desc(i).wait_send()
-
-            each(0, 10, one)
+            for i in range(9):
+                desc(i).wait_send()
             third(1).wait_send()
             third(-1).wait_send()
             fourth().wait_send()
 
-        return lambda: each(0, 10, near_one), forward, arrive, finish
+        return start, forward, arrive, finish
 
     h_start, h_forward, h_arrive, h_finish = spread(gh, hss, hrs)
     d_start, d_forward, d_arrive, d_finish = spread(gd, dss, drs)
@@ -302,7 +298,7 @@
         slot = xl * 8 + z
 
         def desc(k, j):
-            zt = lax.rem(z + j, 8)
+            zt = (z + j) & 7
             return remote(
                 src.at[k, zt], dst.at[slot], ss.at[k * 8 + j], rs.at[slot], (gx - c + k, c * 8 + zt)
             )
@@ -354,19 +350,9 @@
     def own(x):
         return rows(x[:, pl.ds(c, 1)])
 
-    stores = [
-        pltpu.make_async_copy(src, dst, wsem.at[n])
-        for n, (src, dst) in enumerate(
-            [
-                (act_out.at[0], out), (act_out.at[1], ig),
-                (w_out.at[0], gate_grad), (w_out.at[1], up_grad), (w_out.at[2], down_grad),
-            ]
-        )
-    ]
-    w_out[2] = (
+    down_grad[...] = (
         mm_tn(gh[...].reshape(128, 576), own(xc)) + mm_tn(ghp[...].reshape(128, 576), rows(xw[1]))
     ).astype(BF16)
-    stores[4].start()
 
     d_arrive()
     fwd[3].start()
@@ -378,10 +364,8 @@
     both = mm_tn(own(xt), gd[...].reshape(128, 1152)) + mm_tn(
         rows(xw[0]), gdp[...].reshape(128, 1152)
     )
-    w_out[0] = both[:, :576].astype(BF16)
-    w_out[1] = both[:, 576:].astype(BF16)
-    stores[2].start()
-    stores[3].start()
+    gate_grad[...] = both[:, :576].astype(BF16)
+    up_grad[...] = both[:, 576:].astype(BF16)
 
     def summed(ref):
         t = ref[0].astype(F32)
@@ -390,45 +374,36 @@
         return jnp.concatenate([t[:, :576], t[:, 576:]], axis=0).astype(BF16)
 
     o_arrive()
-    act_out[0] = summed(ro)
-    stores[0].start()
+    out[...] = summed(ro)
     for copy in wcopies + fwd:
         copy.wait_send()
     for finish in (tok_finish, cot_finish, gu_finish, hg_finish, h_finish, d_finish, o_finish):
         finish()
     i_arrive()
-    act_out[1] = summed(ri)
-    stores[1].start()
+    ig[...] = summed(ri)
     i_finish()
-    for copy in stores:
-        copy.wait()
 
 
 def write_back(*refs):
-    ins, outs, bufs, get, put = refs[:5], refs[5:10], refs[10:15], refs[15], refs[16]
-    parts = [(n, slice(None)) for n in range(2)]
-    parts += [(n, pl.ds(r * 192, 192)) for r in range(3) for n in range(2, 5)]
-    reads = [pltpu.make_async_copy(ins[n].at[r], bufs[n].at[r], get.at[i]) for i, (n, r) in enumerate(parts)]
-    writes = [pltpu.make_async_copy(bufs[n].at[r], outs[n].at[r], put.at[i]) for i, (n, r) in enumerate(parts)]
-    for copy in reads:
+    copies = [pltpu.make_async_copy(refs[n], refs[5 + n], refs[10].at[n]) for n in range(5)]
+    for copy in copies:
         copy.start()
-    for read, write in zip(reads, writes):
-        read.wait()
-        write.start()
-    for copy in writes:
+    for copy in copies:
         copy.wait()
 
 
 def shards(tokens, gate_weight, up_weight, down_weight, cotangent):
     hbm = pl.BlockSpec(memory_space=pltpu.HBM)
+    vmem = pl.BlockSpec(memory_space=pltpu.VMEM)
     dma = pltpu.SemaphoreType.DMA
     act = jax.ShapeDtypeStruct((16, 576), BF16)
     weight = jax.ShapeDtypeStruct((576, 576), BF16)
-    results = pl.pallas_call(
+    results = (act, act, weight, weight, weight)
+    held = pl.pallas_call(
         kernel,
-        out_shape=(act, act, weight, weight, weight),
+        out_shape=tuple(pltpu.VMEM(t.shape, BF16) for t in results),
         in_specs=[hbm] * 5,
-        out_specs=(hbm,) * 5,
+        out_specs=(vmem,) * 5,
         scratch_shapes=[
             pltpu.VMEM((2, 16, 576), BF16),
             pltpu.VMEM((2, 8, 1152), BF16),
@@ -453,10 +428,8 @@
             pltpu.VMEM((2, 8, 8, 1152), BF16),
             pltpu.VMEM((16, 8, 1152), BF16),
             pltpu.VMEM((16, 8, 1152), BF16),
-            pltpu.VMEM((2, 16, 576), BF16),
-            pltpu.VMEM((3, 576, 576), BF16),
             pltpu.SemaphoreType.REGULAR,
-            dma((5,)), dma((5,)),
+            dma((5,)),
             dma((3,)), dma((3,)),
             dma((14,)), dma((20,)), dma((14,)), dma((20,)),
             dma((16,)), dma((16,)), dma((16,)), dma((16,)),
@@ -465,7 +438,7 @@
             dma((4,)), dma((4,)),
         ],
         compiler_params=pltpu.CompilerParams(
-            collective_id=0, has_side_effects=True, vmem_limit_bytes=64 * 1024 * 1024
+            collective_id=0, has_side_effects=True, vmem_limit_bytes=64_700_000
         ),
         cost_estimate=pl.CostEstimate(
             flops=9 * 2 * 256 * 576 * 576, bytes_accessed=6 * 576 * 576 * 2, transcendentals=8 * 576
@@ -473,13 +446,12 @@
     )(tokens, gate_weight, up_weight, down_weight, cotangent)
     return pl.pallas_call(
         write_back,
-        out_shape=(act, act, weight, weight, weight),
-        in_specs=[hbm] * 5,
+        out_shape=results,
+        in_specs=[vmem] * 5,
         out_specs=(hbm,) * 5,
-        scratch_shapes=[pltpu.VMEM(t.shape, BF16) for t in (act, act, weight, weight, weight)]
-        + [dma((11,)), dma((11,))],
-        compiler_params=pltpu.CompilerParams(vmem_limit_bytes=64 * 1024 * 1024),
-    )(*results)
+        scratch_shapes=[dma((5,))],
+        compiler_params=pltpu.CompilerParams(vmem_limit_bytes=4 * 1024 * 1024),
+    )(*held)
 
 
 def solution(mesh):

time: 68.8 us -> 65.1 us (0.946)
  Pallas kernels: 68 us -> 64.4 us
    pallas_call x2, Pallas kernels: 68 us -> 64.4 us  [the longest x1 62.9 us: shards(): pl.pallas_call(kernel, out_shape=tuple((pltpu.VMEM(t.shape, BF16) for t i...]
where the time goes in v3:
time: 65.1 us; the launch traced here: 65 us
  Pallas kernels  64.4 us (99%)
    pallas_call x1, Pallas kernels, shards(): pl.pallas_call(kernel, out_shape=tuple((pltpu.VMEM(t.shape, BF16) for t i...  62.9 us
    pallas_call x1, Pallas kernels, shards(): pl.pallas_call(write_back, out_shape=results, in_specs=[vmem] * 5, out_sp...  1.41 us

profile of v3, /device:TPU:1, one launch (start us, length us, event | category | flops | bytes accessed | tf_op | source)
XLA Modules:
  0.0 65.0 jit_solution(13120354813765451071)
XLA Ops:
  0.6 62.9 %shard_map.92 = (bf16[16,576]{1,0:T(8,128)(2,1)S(1)}, bf16[16,576]{1,0:T(8,128)(2,1)S(1)}, bf16[576,576]{1,0:T(8,128)(2,1)S(1)}, bf16[576,576]{1,0:T(8,128)(2,1)S(1)}, bf16[576,576]{1,0:T(8,128)(2,1)S(1)}) custom-call(bf16[16,576]{1,0:T(8,128)(2,1)} %tok.1, bf16[576,576]{1,0:T(8,128)(2,1)} %wg.1, bf16[576,576]{1,0:T(8,128)(2,1)} %wu.1, bf16[576,576]{1,0:T(8,128)(2,1)} %wd.1, ...), custom_call_target="tpu_custom_call" | custom-call | flops 1528823808 | bytes 3981312 | tf_op jit(solution)/shard_map/pallas_call | solution.py:402
  63.6 1.4 %shard_map.93 = (bf16[16,576]{1,0:T(8,128)(2,1)}, bf16[16,576]{1,0:T(8,128)(2,1)}, bf16[576,576]{1,0:T(8,128)(2,1)}, bf16[576,576]{1,0:T(8,128)(2,1)}, bf16[576,576]{1,0:T(8,128)(2,1)}) custom-call(bf16[16,576]{1,0:T(8,128)(2,1)S(1)} %get-tuple-element.10.refs_0_, bf16[16,576]{1,0:T(8,128)(2,1)S(1)} %get-tuple-element.11.refs_1_, ...), custom_call_target="tpu_custom_call" | custom-call | tf_op jit(solution)/shard_map/pallas_call | solution.py:447

commit v4 on v3

--- a/solution.py
+++ b/solution.py
@@ -6,6 +6,7 @@
 from jax.sharding import PartitionSpec as P
 
 MESH = pl.DeviceIdType.MESH
+FAR_FIRST = [(d, dx) for d in (4, 3, 5, 2, 6, 1, 7, 0) for dx in (1, 0) if d or dx]
 F32 = jnp.float32
 BF16 = jnp.bfloat16
 
@@ -186,7 +187,7 @@
             return remote(src.at[t], dst.at[i], ss.at[i], rs.at[i], row_dev(dx, dy))
 
         return (
-            lambda: each(1, 16, lambda i: desc(i).start()),
+            lambda: [desc(d * 2 + dx).start() for d, dx in FAR_FIRST],
             lambda: each(1, 16, lambda i: desc(i).wait_recv()),
             lambda: each(1, 16, lambda i: desc(i).wait_send()),
         )
@@ -271,7 +272,21 @@
 
         return start, forward, arrive, finish
 
-    h_start, h_forward, h_arrive, h_finish = spread(gh, hss, hrs)
+    def spread_direct(buf, ss, rs):
+        def desc(dx, dy):
+            return remote(buf.at[me], buf.at[me], ss.at[dy * 2 + dx], rs.at[me], row_dev(dx, dy))
+
+        def here(i):
+            t = ((y + (i >> 1)) & 7) * 2 + ((xh + i) & 1)
+            remote(buf.at[me], buf.at[t], ss.at[0], rs.at[t], peer).wait_recv()
+
+        return (
+            lambda: [desc(dx, dy).start() for dy, dx in FAR_FIRST],
+            lambda: each(1, 16, here),
+            lambda: [desc(dx, dy).wait_send() for dy, dx in FAR_FIRST],
+        )
+
+    h_start, h_arrive, h_finish = spread_direct(gh, hss, hrs)
     d_start, d_forward, d_arrive, d_finish = spread(gd, dss, drs)
 
     gu_arrive()
@@ -291,8 +306,6 @@
         hgrad += rhg[i].astype(F32)
     gd[me] = (jnp.concatenate([hgrad, hgrad], axis=1) * both).astype(BF16)
     d_start()
-    h_forward()
-    d_forward()
 
     def deliver(src, dst, ss, rs):
         slot = xl * 8 + z
@@ -307,16 +320,16 @@
             return (xl == c) & (c == k) & (j == 0)
 
         def start(k):
-            def one(j):
-                @pl.when(is_self(k, j))
-                def _():
-                    pltpu.make_async_copy(src.at[k, z], dst.at[slot], rs.at[slot]).start()
-
-                @pl.when(jnp.logical_not(is_self(k, j)))
-                def _():
-                    desc(k, j).start()
-
-            each(0, 8, one)
+            for j in (4, 3, 5, 2, 6, 1, 7):
+                desc(k, j).start()
+
+            @pl.when(is_self(k, 0))
+            def _():
+                pltpu.make_async_copy(src.at[k, z], dst.at[slot], rs.at[slot]).start()
+
+            @pl.when(jnp.logical_not(is_self(k, 0)))
+            def _():
+                desc(k, 0).start()
 
         def arrive():
             each(
@@ -344,6 +357,7 @@
     for k in range(2):
         so[k] = shares(mm(hidden, w[k, 2])).astype(BF16)
         o_start(k)
+    d_forward()
     for copy in fwd[:3]:
         copy.wait_recv()
 
@@ -433,7 +447,7 @@
             dma((3,)), dma((3,)),
             dma((14,)), dma((20,)), dma((14,)), dma((20,)),
             dma((16,)), dma((16,)), dma((16,)), dma((16,)),
-            dma((13,)), dma((19,)), dma((13,)), dma((19,)),
+            dma((16,)), dma((16,)), dma((13,)), dma((19,)),
             dma((16,)), dma((16,)), dma((16,)), dma((16,)),
             dma((4,)), dma((4,)),
         ],

time: 65.1 us -> 61.3 us (0.942)
  Pallas kernels: 64.4 us -> 60.5 us
    pallas_call x1, Pallas kernels: 62.9 us -> 59.1 us  [shards(): pl.pallas_call(kernel, out_shape=tuple((pltpu.VMEM(t.shape, BF16) for t i...]
where the time goes in v4:
time: 61.3 us; the launch traced here: 61.2 us
  Pallas kernels  60.5 us (99%)
  between operations  0.64 us (1%)
    pallas_call x1, Pallas kernels, shards(): pl.pallas_call(kernel, out_shape=tuple((pltpu.VMEM(t.shape, BF16) for t i...  59.1 us
    pallas_call x1, Pallas kernels, shards(): pl.pallas_call(write_back, out_shape=results, in_specs=[vmem] * 5, out_sp...  1.41 us

profile of v4, /device:TPU:1, one launch (start us, length us, event | category | flops | bytes accessed | tf_op | source)
XLA Modules:
  0.0 61.2 jit_solution(16778086559617565349)
XLA Ops:
  0.6 59.1 %shard_map.92 = (bf16[16,576]{1,0:T(8,128)(2,1)S(1)}, bf16[16,576]{1,0:T(8,128)(2,1)S(1)}, bf16[576,576]{1,0:T(8,128)(2,1)S(1)}, bf16[576,576]{1,0:T(8,128)(2,1)S(1)}, bf16[576,576]{1,0:T(8,128)(2,1)S(1)}) custom-call(bf16[16,576]{1,0:T(8,128)(2,1)} %tok.1, bf16[576,576]{1,0:T(8,128)(2,1)} %wg.1, bf16[576,576]{1,0:T(8,128)(2,1)} %wu.1, bf16[576,576]{1,0:T(8,128)(2,1)} %wd.1, ...), custom_call_target="tpu_custom_call" | custom-call | flops 1528823808 | bytes 3981312 | tf_op jit(solution)/shard_map/pallas_call | solution.py:416
  59.8 1.4 %shard_map.93 = (bf16[16,576]{1,0:T(8,128)(2,1)}, bf16[16,576]{1,0:T(8,128)(2,1)}, bf16[576,576]{1,0:T(8,128)(2,1)}, bf16[576,576]{1,0:T(8,128)(2,1)}, bf16[576,576]{1,0:T(8,128)(2,1)}) custom-call(bf16[16,576]{1,0:T(8,128)(2,1)S(1)} %get-tuple-element.10.refs_0_, bf16[16,576]{1,0:T(8,128)(2,1)S(1)} %get-tuple-element.11.refs_1_, ...), custom_call_target="tpu_custom_call" | custom-call | tf_op jit(solution)/shard_map/pallas_call | solution.py:461

commit v5 on v4

--- a/solution.py
+++ b/solution.py
@@ -287,7 +287,7 @@
         )
 
     h_start, h_arrive, h_finish = spread_direct(gh, hss, hrs)
-    d_start, d_forward, d_arrive, d_finish = spread(gd, dss, drs)
+    d_start, d_arrive, d_finish = spread_direct(gd, dss, drs)
 
     gu_arrive()
     total = pgu[me]
@@ -357,7 +357,6 @@
     for k in range(2):
         so[k] = shares(mm(hidden, w[k, 2])).astype(BF16)
         o_start(k)
-    d_forward()
     for copy in fwd[:3]:
         copy.wait_recv()
 
@@ -447,7 +446,7 @@
             dma((3,)), dma((3,)),
             dma((14,)), dma((20,)), dma((14,)), dma((20,)),
             dma((16,)), dma((16,)), dma((16,)), dma((16,)),
-            dma((16,)), dma((16,)), dma((13,)), dma((19,)),
+            dma((16,)), dma((16,)), dma((16,)), dma((16,)),
             dma((16,)), dma((16,)), dma((16,)), dma((16,)),
             dma((4,)), dma((4,)),
         ],

time: 61.3 us -> 61.5 us (level)
  no operation moved by 1% of the time
where the time goes in v5:
time: 61.5 us; the launch traced here: 61.4 us
  Pallas kernels  60.8 us (99%)
  between operations  0.64 us (1%)
    pallas_call x1, Pallas kernels, shards(): pl.pallas_call(kernel, out_shape=tuple((pltpu.VMEM(t.shape, BF16) for t i...  59.4 us
    pallas_call x1, Pallas kernels, shards(): pl.pallas_call(write_back, out_shape=results, in_specs=[vmem] * 5, out_sp...  1.41 us

profile of v5, /device:TPU:1, one launch (start us, length us, event | category | flops | bytes accessed | tf_op | source)
XLA Modules:
  0.0 61.4 jit_solution(17353737448509306527)
XLA Ops:
  0.6 59.4 %shard_map.92 = (bf16[16,576]{1,0:T(8,128)(2,1)S(1)}, bf16[16,576]{1,0:T(8,128)(2,1)S(1)}, bf16[576,576]{1,0:T(8,128)(2,1)S(1)}, bf16[576,576]{1,0:T(8,128)(2,1)S(1)}, bf16[576,576]{1,0:T(8,128)(2,1)S(1)}) custom-call(bf16[16,576]{1,0:T(8,128)(2,1)} %tok.1, bf16[576,576]{1,0:T(8,128)(2,1)} %wg.1, bf16[576,576]{1,0:T(8,128)(2,1)} %wu.1, bf16[576,576]{1,0:T(8,128)(2,1)} %wd.1, ...), custom_call_target="tpu_custom_call" | custom-call | flops 1528823808 | bytes 3981312 | tf_op jit(solution)/shard_map/pallas_call | solution.py:415
  60.0 1.4 %shard_map.93 = (bf16[16,576]{1,0:T(8,128)(2,1)}, bf16[16,576]{1,0:T(8,128)(2,1)}, bf16[576,576]{1,0:T(8,128)(2,1)}, bf16[576,576]{1,0:T(8,128)(2,1)}, bf16[576,576]{1,0:T(8,128)(2,1)}) custom-call(bf16[16,576]{1,0:T(8,128)(2,1)S(1)} %get-tuple-element.10.refs_0_, bf16[16,576]{1,0:T(8,128)(2,1)S(1)} %get-tuple-element.11.refs_1_, ...), custom_call_target="tpu_custom_call" | custom-call | tf_op jit(solution)/shard_map/pallas_call | solution.py:460
